TPU v7x, 128 devices: a whole 4x4x4 slice. The times are simulated.
128 devices in a mesh: row: 8 (over y, x_hi), col: 16 (over x_lo, z, core).
Axes of the slice: x: 4 (x_hi: 2, x_lo: 2; x = x_hi * 2 + x_lo), y: 4, z: 4, core: 2. Of those that a mesh axis runs over, the one named last changes fastest.
Arguments:
- alignment: float32 [512, 512, 256], P('row', 'col'), may hold values from -6 to 6
- align_gain: float32 [256], replicated, may hold values from 0.5 to 1.5
- align_bias: float32 [256], replicated, may hold values from -1.75 to 1.75
- left_weight: float32 [256, 32], replicated, may hold values from -0.375 to 0.375
- right_weight: float32 [256, 32], replicated, may hold values from -0.375 to 0.375
- project_weight: float32 [1024, 128], replicated, may hold values from -3 to 3
- project_bias: float32 [128], replicated, may hold values from -1.75 to 1.75
- pair_state: float32 [512, 512, 128], P('row', 'col'), may hold values from -6 to 6
- pair_gain: float32 [128], replicated, may hold values from 0.5 to 1.5
- pair_bias: float32 [128], replicated, may hold values from -1.75 to 1.75
- hidden_weight: float32 [128, 512], replicated, may hold values from -0.5 to 0.5
- hidden_bias: float32 [512], replicated, may hold values from -1.75 to 1.75
- final_weight: float32 [512, 128], replicated, may hold values from -0.25 to 0.25
- final_bias: float32 [128], replicated, may hold values from -1.75 to 1.75
Outputs:
- pair_next: float32 [512, 512, 128], P('row', 'col')
All inputs are finite; a program needn't handle non-finite values.
Results may differ from a plain program's by a relative error of at most 0.0003.
Values sent between devices are 32-bit elements; how exact they have to be, the bound alone decides.
A program may use at most 128 MiB of HBM per device.

v0:
```python
import functools

import jax
import jax.numpy as jnp
from jax import lax
from jax.experimental import pallas as pl
from jax.experimental.pallas import tpu as pltpu
from jax.sharding import PartitionSpec as P

F32 = jnp.float32
BF16 = jnp.bfloat16
MESH = pl.DeviceIdType.MESH
CH = 4


def split(value):
    high = value.astype(BF16)
    low = (value - high.astype(F32)).astype(BF16)
    return high, low


def dot(a, b):
    return jnp.dot(a, b, preferred_element_type=F32)


def center(values, width):
    total = values[0]
    for part in values[1:]:
        total = total + part
    middle = jnp.sum(total, axis=-1, keepdims=True) * (1.0 / width)
    values = [part - middle for part in values]
    total = values[0] * values[0]
    for part in values[1:]:
        total = total + part * part
    spread = jnp.sum(total, axis=-1, keepdims=True) * (1.0 / width)
    factor = lax.rsqrt(spread + 1e-05)
    return [part * factor for part in values]


def kernel(
    align,
    gain_ref,
    offset_ref,
    lw_ref,
    rw_ref,
    pw_hbm,
    pbias_ref,
    pair_hbm,
    pgain_ref,
    poffset_ref,
    hw_ref,
    hbias_ref,
    fw_ref,
    fbias_ref,
    out_hbm,
    x0,
    x1,
    xh,
    xl,
    wh,
    wl,
    send_left,
    left,
    right,
    lhs,
    rhs,
    raw,
    oh,
    ol,
    pw,
    pwc,
    hwc,
    fwc,
    pair,
    out,
    load_sem,
    r_send,
    r_recv,
    l_send,
    l_recv,
    c_send,
    c_recv,
    t_send,
    t_recv,
    out_sem,
):
    row, col = lax.axis_index("row"), lax.axis_index("col")
    y, x_hi = row // 2, row % 2
    k, core = col // 2, col % 2
    x_lo, z = k // 4, k % 4

    def at_row(y_, x_):
        return (y_ % 4) * 2 + x_

    def at_k(x_, z_):
        return x_ * 4 + z_ % 4

    def same_col(r):
        return (r, col)

    def same_row(k_):
        return (row, k_ * 2 + core)

    other_core = (row, k * 2 + 1 - core)
    swap = (k, row * 2 + core)
    y_up, y_down = same_col(at_row(y + 1, x_hi)), same_col(at_row(y + 3, x_hi))
    x_far = same_col(at_row(y, 1 - x_hi))
    z_up, z_down = same_row(at_k(x_lo, z + 1)), same_row(at_k(x_lo, z + 3))
    x_near = same_row(at_k(1 - x_lo, z))
    stays = k == row

    loads = [
        pltpu.make_async_copy(align.at[:, pl.ds(0, 128)], x0, load_sem.at[0]),
        pltpu.make_async_copy(align.at[:, pl.ds(128, 128)], x1, load_sem.at[1]),
        pltpu.make_async_copy(pw_hbm, pw, load_sem.at[2]),
        pltpu.make_async_copy(pair_hbm, pair, load_sem.at[3]),
    ]
    for load in loads:
        load.start()

    barrier = pltpu.get_barrier_semaphore()
    for device in (other_core, y_up, y_down, x_far, z_up, z_down, x_near):
        pl.semaphore_signal(barrier, inc=1, device_id=device, device_id_type=MESH)

    @pl.when(jnp.logical_not(stays))
    def _():
        pl.semaphore_signal(barrier, inc=1, device_id=swap, device_id_type=MESH)

    lane = lax.broadcasted_iota(jnp.int32, (256, 128), 1)
    for source, at in ((lw_ref, 0), (rw_ref, 128)):
        wide = jnp.concatenate([source[...]] * 4, axis=1)
        for pos in range(4):
            placed = jnp.where(lane // 32 == pos, wide, 0.0)
            high, low = split(placed)
            wh[pl.ds(pos * 256, 256), pl.ds(at, 128)] = high
            wl[pl.ds(pos * 256, 256), pl.ds(at, 128)] = low

    loads[0].wait()
    loads[1].wait()

    gain = gain_ref[...]
    offset = offset_ref[...]

    def norm_body(g, carry):
        for pos in range(4):
            rows = pl.ds(g * 4 + pos, 64, stride=32)
            parts = center([x0[rows, :], x1[rows, :]], 256)
            for half in range(2):
                value = parts[half] * gain[:, half * 128 : half * 128 + 128] + offset[:, half * 128 : half * 128 + 128]
                high, low = split(value)
                at = pl.ds(pl.multiple_of(g * 64, 64), 64)
                xh[at, pl.ds(pos * 256 + half * 128, 128)] = high
                xl[at, pl.ds(pos * 256 + half * 128, 128)] = low
        return carry

    lax.fori_loop(0, 8, norm_body, 0)
    both = dot(xh[...], wh[...]) + dot(xl[...], wh[...]) + dot(xh[...], wl[...])
    for g in range(8):
        send_left[g // 2, :, pl.ds((g % 2) * 128, 128)] = both[g * 64 : g * 64 + 64, :128]
    for g in range(4):
        pair_rows = jnp.concatenate(
            [both[g * 64 : g * 64 + 64, 128:], both[g * 64 + 256 : g * 64 + 320, 128:]], axis=0
        )
        right[row, pl.ds(g * 128, 128), :] = pair_rows.T

    @pl.when(jnp.logical_not(stays))
    def _():
        pl.semaphore_wait(barrier, 8)

    @pl.when(stays)
    def _():
        pl.semaphore_wait(barrier, 7)

    def r_copy(step, n, slot, device):
        block = right.at[slot, pl.ds(n * 128, 128), :]
        return pltpu.make_async_remote_copy(
            src_ref=block,
            dst_ref=block,
            send_sem=r_send.at[step, n],
            recv_sem=r_recv.at[step, n],
            device_id=device,
            device_id_type=MESH,
        )

    def l_copy(step, n, slot, device):
        block = left.at[n, core, slot]
        return pltpu.make_async_remote_copy(
            src_ref=block,
            dst_ref=block,
            send_sem=l_send.at[step, n],
            recv_sem=l_recv.at[step, n],
            device_id=device,
            device_id_type=MESH,
        )

    def c_copy(step, n, slot, half):
        block = left.at[n, half, slot]
        return pltpu.make_async_remote_copy(
            src_ref=block,
            dst_ref=block,
            send_sem=c_send.at[step, n],
            recv_sem=c_recv.at[step, n],
            device_id=other_core,
            device_id_type=MESH,
        )

    def t_copy(n):
        return pltpu.make_async_remote_copy(
            src_ref=send_left.at[n],
            dst_ref=left.at[n, core, row],
            send_sem=t_send.at[n],
            recv_sem=t_recv.at[n],
            device_id=swap,
            device_id_type=MESH,
        )

    def t_arrival(n):
        return pltpu.make_async_copy(send_left.at[n], left.at[n, core, k], t_recv.at[n])

    r_sent = [row, row, row, at_row(y, 1 - x_hi), at_row(y, 1 - x_hi), at_row(y + 3, x_hi), at_row(y + 1, 1 - x_hi)]
    r_to = [x_far, y_up, y_down, y_up, y_down, y_up, y_down]
    r_lands = [
        at_row(y, 1 - x_hi),
        at_row(y + 3, x_hi),
        at_row(y + 1, x_hi),
        at_row(y + 3, 1 - x_hi),
        at_row(y + 1, 1 - x_hi),
        at_row(y + 2, x_hi),
        at_row(y + 2, 1 - x_hi),
    ]
    l_sent = [k, k, k, at_k(1 - x_lo, z), at_k(1 - x_lo, z), at_k(x_lo, z + 3), at_k(1 - x_lo, z + 1)]
    l_to = [x_near, z_up, z_down, z_up, z_down, z_up, z_down]
    l_lands = [
        at_k(1 - x_lo, z),
        at_k(x_lo, z + 3),
        at_k(x_lo, z + 1),
        at_k(1 - x_lo, z + 3),
        at_k(1 - x_lo, z + 1),
        at_k(x_lo, z + 2),
        at_k(1 - x_lo, z + 2),
    ]
    c_slots = [k] + l_lands

    def r_start(step, n):
        r_copy(step, n, r_sent[step], r_to[step]).start()

    def r_wait(step, n):
        r_copy(step, n, r_lands[step], r_to[step]).wait_recv()

    def l_start(step, n):
        l_copy(step, n, l_sent[step], l_to[step]).start()

    def l_wait(step, n):
        l_copy(step, n, l_lands[step], l_to[step]).wait_recv()

    def c_start(step, n):
        c_copy(step, n, c_slots[step], core).start()

    def c_wait(step, n):
        c_copy(step, n, c_slots[step], 1 - core).wait_recv()

    for n in range(CH):

        @pl.when(jnp.logical_not(stays))
        def _(n=n):
            t_copy(n).start()

        @pl.when(stays)
        def _(n=n):
            t_arrival(n).start()

        for step in (1, 2, 0):
            r_start(step, n)

    loads[2].wait()

    def order_body(d, carry):
        high, low = split(pw[pl.ds(d, 32, stride=32), :])
        at = pl.ds(pl.multiple_of(d * 32, 32), 32)
        pwc[at, pl.ds(0, 128)] = high
        pwc[at, pl.ds(128, 128)] = low
        return carry

    lax.fori_loop(0, 32, order_body, 0)
    high, low = split(hw_ref[...])
    hwc[pl.ds(0, 128), :] = high
    hwc[pl.ds(128, 128), :] = high
    hwc[pl.ds(256, 128), :] = low
    high, low = split(fw_ref[...])
    fwc[:, pl.ds(0, 128)] = high
    fwc[:, pl.ds(128, 128)] = low

    def wave_a(n):
        t_arrival(n).wait()
        for step in (0, 1, 2):
            l_start(step, n)
        c_start(0, n)

    def wave_b(n):
        l_wait(0, n)
        l_start(3, n)
        l_start(4, n)
        c_start(1, n)
        r_wait(0, n)
        r_start(3, n)
        r_start(4, n)

    def wave_c(n):
        r_wait(1, n)
        r_start(5, n)
        l_wait(1, n)
        l_start(5, n)
        c_start(2, n)
        l_wait(2, n)
        c_start(3, n)

    def wave_d(n):
        r_wait(4, n)
        r_start(6, n)
        l_wait(4, n)
        l_start(6, n)
        c_start(5, n)
        l_wait(3, n)
        c_start(4, n)

    def wave_e(n):
        l_wait(5, n)
        c_start(6, n)
        l_wait(6, n)
        c_start(7, n)

    waves = [wave_a, wave_b, wave_c, wave_d, wave_e]
    for turn in range(CH + len(waves) - 1):
        for at, wave in enumerate(waves):
            if 0 <= turn - at < CH:
                wave(turn - at)
    for n in range(CH):
        for step in (2, 3, 5, 6):
            r_wait(step, n)

    low_half = lax.broadcasted_iota(jnp.int32, (16, 128), 1) < 64

    def right_body(d, carry):
        first, second = [], []
        for p in range(4):
            a = right[2 * p, pl.ds(d, 16, stride=32), :]
            b = right[2 * p + 1, pl.ds(d, 16, stride=32), :]
            first.append(jnp.where(low_half, a, pltpu.roll(b, 64, 1)))
            second.append(jnp.where(low_half, pltpu.roll(a, 64, 1), b))
        for at, parts in enumerate((first, second)):
            rows = pl.ds(pl.multiple_of(d * 32 + at * 16, 16), 16)
            for p in range(4):
                high, low = split(parts[p])
                lhs[rows, pl.ds(p * 128, 128)] = high
                lhs[rows, pl.ds(512 + p * 128, 128)] = low
                lhs[rows, pl.ds(1024 + p * 128, 128)] = high
        return carry

    lax.fori_loop(0, 32, right_body, 0)
    loads[3].wait()

    lane = lax.broadcasted_iota(jnp.int32, (32, 128), 1)
    below = lane < 64
    even = (lane // 32) % 2 == 0
    pbias, fbias, hbias = pbias_ref[...], fbias_ref[...], hbias_ref[...]
    pgain, poffset = pgain_ref[...], poffset_ref[...]

    def exchange_halves(a, b):
        moved = pltpu.roll(jnp.where(below, b, a), 64, 1)
        return jnp.where(below, a, moved), jnp.where(below, moved, b)

    def exchange_quarters(a, b):
        return jnp.where(even, a, pltpu.roll(b, 32, 1)), jnp.where(even, pltpu.roll(a, 96, 1), b)

    def tile_body(m, carry):
        q, h = m // 2, m % 2
        piece = left[q, h].reshape(512, 256)
        high, low = split(piece)
        rhs[pl.ds(0, 512), :] = high
        rhs[pl.ds(512, 512), :] = high
        rhs[pl.ds(1024, 512), :] = low
        raw[...] = dot(lhs[...], rhs[...])
        for t in range(8):
            for u in range(2):
                v = [raw[pl.ds((4 * t + d) * 32, 32), pl.ds(u * 128, 128)] for d in range(4)]
                v[0], v[2] = exchange_halves(v[0], v[2])
                v[1], v[3] = exchange_halves(v[1], v[3])
                v[0], v[1] = exchange_quarters(v[0], v[1])
                v[2], v[3] = exchange_quarters(v[2], v[3])
                for i in range(4):
                    high, low = split(v[i])
                    oh[pl.ds((u * 4 + i) * 32, 32), pl.ds(t * 128, 128)] = high
                    ol[pl.ds((u * 4 + i) * 32, 32), pl.ds(t * 128, 128)] = low
        wide = dot(oh[...], pwc[...])
        update = wide[:, :128] + wide[:, 128:] + dot(ol[...], pwc[:, :128])
        rows = pl.ds(pl.multiple_of((h * 32 + q * 8) * 32, 256), 256)
        updated = pair[rows, :] + update * (1.0 / 512) + pbias
        (flat,) = center([updated], 128)
        high, low = split(flat * pgain + poffset)
        hidden = jnp.maximum(dot(jnp.concatenate([high, low, high], axis=1), hwc[...]) + hbias, 0.0)
        high, low = split(hidden)
        wide = dot(high, fwc[...])
        final = wide[:, :128] + wide[:, 128:] + dot(low, fwc[:, :128])
        out[rows, :] = updated + final + fbias
        return carry

    def step_body(m, carry):
        q, h = m // 2, m % 2

        @pl.when(h == 0)
        def _():
            for step in range(8):
                c_wait(step, q)

        tile_body(m, carry)
        rows = pl.ds(pl.multiple_of((h * 32 + q * 8) * 32, 256), 256)
        pltpu.make_async_copy(out.at[rows, :], out_hbm.at[rows, :], out_sem.at[m]).start()
        return carry

    lax.fori_loop(0, 8, step_body, 0)

    def out_wait(m, carry):
        q, h = m // 2, m % 2
        rows = pl.ds(pl.multiple_of((h * 32 + q * 8) * 32, 256), 256)
        pltpu.make_async_copy(out.at[rows, :], out_hbm.at[rows, :], out_sem.at[m]).wait()
        return carry

    lax.fori_loop(0, 8, out_wait, 0)
    for n in range(CH):
        for step in range(7):
            r_copy(step, n, r_sent[step], r_to[step]).wait_send()
            l_copy(step, n, l_sent[step], l_to[step]).wait_send()
        for step in range(8):
            c_copy(step, n, c_slots[step], core).wait_send()

        @pl.when(jnp.logical_not(stays))
        def _(n=n):
            t_copy(n).wait_send()


def on_device(
    alignment,
    align_gain,
    align_bias,
    left_weight,
    right_weight,
    project_weight,
    project_bias,
    pair_state,
    pair_gain,
    pair_bias,
    hidden_weight,
    hidden_bias,
    final_weight,
    final_bias,
):
    whole = pl.BlockSpec(memory_space=pltpu.VMEM)
    apart = pl.BlockSpec(memory_space=pl.ANY)
    dma = pltpu.SemaphoreType.DMA
    output = pl.pallas_call(
        kernel,
        out_shape=jax.ShapeDtypeStruct((2048, 128), F32),
        in_specs=[apart, whole, whole, whole, whole, apart, whole, apart] + [whole] * 6,
        out_specs=apart,
        scratch_shapes=[
            pltpu.VMEM((2048, 128), F32),
            pltpu.VMEM((2048, 128), F32),
            pltpu.VMEM((512, 1024), BF16),
            pltpu.VMEM((512, 1024), BF16),
            pltpu.VMEM((1024, 256), BF16),
            pltpu.VMEM((1024, 256), BF16),
            pltpu.VMEM((CH, 64, 256), F32),
            pltpu.VMEM((CH, 2, 8, 64, 256), F32),
            pltpu.VMEM((8, 512, 128), F32),
            pltpu.VMEM((1024, 1536), BF16),
            pltpu.VMEM((1536, 256), BF16),
            pltpu.VMEM((1024, 256), F32),
            pltpu.VMEM((256, 1024), BF16),
            pltpu.VMEM((256, 1024), BF16),
            pltpu.VMEM((1024, 128), F32),
            pltpu.VMEM((1024, 256), BF16),
            pltpu.VMEM((384, 512), BF16),
            pltpu.VMEM((512, 256), BF16),
            pltpu.VMEM((2048, 128), F32),
            pltpu.VMEM((2048, 128), F32),
            dma((4,)),
            dma((7, CH)),
            dma((7, CH)),
            dma((7, CH)),
            dma((7, CH)),
            dma((8, CH)),
            dma((8, CH)),
            dma((CH,)),
            dma((CH,)),
            dma((8,)),
        ],
        compiler_params=pltpu.CompilerParams(
            collective_id=0, has_side_effects=True, vmem_limit_bytes=48 * 1024 * 1024
        ),
        cost_estimate=pl.CostEstimate(flops=10**10, bytes_accessed=6 * 10**6, transcendentals=0),
    )(
        alignment.reshape(2048, 256),
        align_gain.reshape(1, 256),
        align_bias.reshape(1, 256),
        left_weight,
        right_weight,
        project_weight,
        project_bias.reshape(1, 128),
        pair_state.reshape(2048, 128),
        pair_gain.reshape(1, 128),
        pair_bias.reshape(1, 128),
        hidden_weight,
        hidden_bias.reshape(1, 512),
        final_weight,
        final_bias.reshape(1, 128),
    )
    return output.reshape(64, 32, 128)


def solution(mesh):
    spread = P("row", "col", None)
    placed = (spread,) + (P(),) * 6 + (spread,) + (P(),) * 6
    return jax.shard_map(on_device, mesh=mesh, in_specs=placed, out_specs=spread, check_vma=False)
```

profile of v0, /device:TPU:10, one launch (start us, length us, event | category | flops | bytes accessed | tf_op | source)
XLA Modules:
  0.0 94.5 jit_solution(13471402466928368827)
XLA Ops:
  0.0 0.9 copy.15.lw_ref
  0.9 0.9 copy.16.rw_ref
  1.7 0.0 copy-start
  1.7 1.6 %copy-done = f32[64,32,256]{2,1,0:T(8,128)S(1)} copy-done((f32[64,32,256]{2,1,0:T(8,128)S(1)}, f32[64,32,256]{2,1,0:T(8,128)}, u32[]{:S(2)}) %copy-start) | copy-done | bytes 2097176
  3.3 0.0 copy-start.1
  3.3 1.2 %copy-done.1 = f32[64,32,128]{2,1,0:T(8,128)S(1)} copy-done((f32[64,32,128]{2,1,0:T(8,128)S(1)}, f32[64,32,128]{2,1,0:T(8,128)}, u32[]{:S(2)}) %copy-start.1) | copy-done | bytes 1048600
  4.5 0.0 copy-start.2
  4.5 1.0 %copy-done.2 = f32[1024,128]{1,0:T(8,128)S(1)} copy-done((f32[1024,128]{1,0:T(8,128)S(1)}, f32[1024,128]{1,0:T(8,128)}, u32[]{:S(2)}) %copy-start.2) | copy-done | bytes 524312
  5.6 0.0 copy-start.3
  5.6 0.9 %copy-done.3 = f32[128,512]{1,0:T(8,128)S(1)} copy-done((f32[128,512]{1,0:T(8,128)S(1)}, f32[128,512]{1,0:T(8,128)}, u32[]{:S(2)}) %copy-start.3) | copy-done | bytes 262168
  6.5 0.0 copy-start.4
  6.5 0.9 %copy-done.4 = f32[512,128]{1,0:T(8,128)S(1)} copy-done((f32[512,128]{1,0:T(8,128)S(1)}, f32[512,128]{1,0:T(8,128)}, u32[]{:S(2)}) %copy-start.4) | copy-done | bytes 262168
  7.5 0.0 copy-start.5
  7.5 0.7 copy-done.5
  8.2 0.0 copy-start.6
  8.2 0.7 copy-done.6
  8.8 0.0 copy-start.7
  8.8 0.7 copy-done.7
  9.5 0.0 copy-start.8
  9.5 0.7 copy-done.8
  10.2 0.0 copy-start.9
  10.2 0.7 copy-done.9
  10.8 0.0 copy-start.10
  10.8 0.7 copy-done.10
  11.5 0.0 copy-start.11
  11.5 0.7 copy-done.11
  12.1 81.4 %shard_map.136 = f32[2048,128]{1,0:T(8,128)S(1)} custom-call(f32[2048,256]{1,0:T(8,128)S(1)} %bitcast.11, f32[1,256]{1,0:T(1,128)S(1)} %bitcast.14, f32[1,256]{1,0:T(1,128)S(1)} %bitcast.15, f32[256,32]{1,0:T(8,128)S(1)} %copy.15.lw_ref, f32[256,32]{1,0:T(8,128)S(1)} %copy.16.rw_ref, f32[1024,128]{1,0:T(8,128)S(1)} %copy-done.2, f32[1,128]{1,0:T(1,128)S(1)} %bitcast.16, ...), custom_call_target="tpu_custom_call" | custom-call | flops 10000000000 | bytes 6000000 | tf_op jit(solution)/shard_map/pallas_call | solution.py:460
  93.6 1.0 %copy.18 = f32[64,32,128]{2,1,0:T(8,128)} copy(f32[64,32,128]{2,1,0:T(8,128)S(1)} %bitcast.10) | data formatting | bytes 2097152
Async XLA Ops:
  1.7 1.6 %copy-start = (f32[64,32,256]{2,1,0:T(8,128)S(1)}, f32[64,32,256]{2,1,0:T(8,128)}, u32[]{:S(2)}) copy-start(f32[64,32,256]{2,1,0:T(8,128)} %param.14) | copy-start | bytes 6291460
  3.3 1.2 %copy-start.1 = (f32[64,32,128]{2,1,0:T(8,128)S(1)}, f32[64,32,128]{2,1,0:T(8,128)}, u32[]{:S(2)}) copy-start(f32[64,32,128]{2,1,0:T(8,128)} %param.21) | copy-start | bytes 3145732
  4.5 1.0 %copy-start.2 = (f32[1024,128]{1,0:T(8,128)S(1)}, f32[1024,128]{1,0:T(8,128)}, u32[]{:S(2)}) copy-start(f32[1024,128]{1,0:T(8,128)} %pw_hbm.1) | copy-start | bytes 1572868
  5.6 0.9 %copy-start.3 = (f32[128,512]{1,0:T(8,128)S(1)}, f32[128,512]{1,0:T(8,128)}, u32[]{:S(2)}) copy-start(f32[128,512]{1,0:T(8,128)} %hw_ref.1) | copy-start | bytes 786436
  6.5 0.9 %copy-start.4 = (f32[512,128]{1,0:T(8,128)S(1)}, f32[512,128]{1,0:T(8,128)}, u32[]{:S(2)}) copy-start(f32[512,128]{1,0:T(8,128)} %fw_ref.1) | copy-start | bytes 786436
  7.5 0.7 copy-start.5
  8.2 0.7 copy-start.6
  8.8 0.7 copy-start.7
  9.5 0.7 copy-start.8
  10.2 0.7 copy-start.9
  10.8 0.7 copy-start.10
  11.5 0.7 copy-start.11
where the time goes:
time: 95 us; the launch traced here: 94.5 us
  Pallas kernels  81.4 us (86%)
  local copies, waits for them, and re-layouts  13.1 us (14%)
    pallas_call x1, Pallas kernels, on_device(): pl.pallas_call(kernel, out_shape=jax.ShapeDtypeStruct((2048, 128), F32),...  81.4 us
    unnamed x27, local copies, waits for them, and re-layouts  13.1 us

commit v1 on v0

v1 whole, which is shorter than its diff:
```python
import functools

import jax
import jax.numpy as jnp
from jax import lax
from jax.experimental import pallas as pl
from jax.experimental.pallas import tpu as pltpu
from jax.sharding import PartitionSpec as P

F32 = jnp.float32
BF16 = jnp.bfloat16
MESH = pl.DeviceIdType.MESH
CH = 4
ORDER = (
    ("r1", 0), ("t1", 0), ("r0", 0), ("r1", 1), ("t1", 1), ("r0", 1), ("r1", 2), ("t1", 2), ("r0", 2),
    ("r1", 3), ("t2", 0), ("t1", 3), ("r0", 3), ("P", 0), ("t2", 1), ("r4", 0), ("t2", 2), ("r4", 1),
    ("l1", 0), ("l2", 0), ("l0", 0), ("t2", 3), ("r4", 2), ("l1", 1), ("l2", 1), ("l0", 1), ("l1", 2),
    ("l2", 2), ("l0", 2), ("r4", 3), ("P", 2), ("l5", 0), ("l4", 0), ("l0", 3), ("l3", 0), ("l2", 3),
    ("l1", 3), ("l4", 1), ("l5", 1), ("l4", 2), ("P", 1), ("P", 3), ("l3", 1), ("l6", 0), ("l5", 2),
    ("l4", 3), ("O", 0), ("l3", 2), ("l6", 1), ("F", 0), ("l3", 3), ("l6", 2), ("l5", 3), ("l6", 3), ("O", 1),
    ("F", 1), ("O", 2), ("F", 2), ("O", 3), ("F", 3),
)


def split(value):
    high = value.astype(BF16)
    low = (value - high.astype(F32)).astype(BF16)
    return high, low


def dot(a, b):
    return jnp.dot(a, b, preferred_element_type=F32)


def center(values, width):
    total = values[0]
    for part in values[1:]:
        total = total + part
    middle = jnp.sum(total, axis=-1, keepdims=True) * (1.0 / width)
    values = [part - middle for part in values]
    total = values[0] * values[0]
    for part in values[1:]:
        total = total + part * part
    spread = jnp.sum(total, axis=-1, keepdims=True) * (1.0 / width)
    factor = lax.rsqrt(spread + 1e-05)
    return [part * factor for part in values]


def kernel(
    align,
    gain_hbm,
    offset_hbm,
    lw_hbm,
    rw_hbm,
    pw_hbm,
    pbias_hbm,
    pair_hbm,
    pgain_hbm,
    poffset_hbm,
    hw_hbm,
    hbias_hbm,
    fw_hbm,
    fbias_hbm,
    out_hbm,
    gain_ref,
    offset_ref,
    lw_ref,
    rw_ref,
    pbias_ref,
    pgain_ref,
    poffset_ref,
    hw_ref,
    hbias_ref,
    fw_ref,
    fbias_ref,
    x0,
    x1,
    xh,
    xl,
    wh,
    wl,
    send_left,
    passing,
    left,
    right,
    lhs,
    rhs,
    raw,
    oh,
    ol,
    pw,
    pwc,
    hwc,
    fwc,
    pair,
    out,
    load_sem,
    r_send,
    r_recv,
    l_send,
    l_recv,
    c_send,
    c_recv,
    t_send,
    t_recv,
    out_sem,
):
    row, col = lax.axis_index("row"), lax.axis_index("col")
    y, x_hi = row // 2, row % 2
    k, core = col // 2, col % 2
    x_lo, z = k // 4, k % 4

    def at_row(y_, x_):
        return (y_ % 4) * 2 + x_

    def at_k(x_, z_):
        return x_ * 4 + z_ % 4

    def same_col(r):
        return (r, col)

    def same_row(k_):
        return (row, k_ * 2 + core)

    other_core = (row, k * 2 + 1 - core)
    t_y = 2 * x_lo + z // 2
    t_x = jnp.where(x_hi == z % 2, x_lo, 1 - x_lo)
    t_z = (z + y - t_y + 4) % 4
    first_to = (y * 2 + z % 2, (t_x * 4 + t_z) * 2 + core)
    mid = (z - y - x_hi + 8) % 4
    mid_x, mid_w = mid // 2, mid % 2
    mid_hi = jnp.where(x_lo == mid_x, x_hi, 1 - x_hi)
    first_from = (y * 2 + mid_hi, (mid_x * 4 + 2 * mid_w + x_hi) * 2 + core)
    mid_shard = y * 2 + mid_hi
    mid_y = 2 * mid_x + mid_w
    second_to = (mid_y * 2 + x_hi, col)

    def shard_at(x_, z_):
        return ((z_ - y % 2 - x_hi + 2 * (y // 2) + 8) % 4) * 2 + jnp.where(x_ == y // 2, x_hi, 1 - x_hi)

    shard = shard_at(x_lo, z)
    second_from = ((shard // 2) * 2 + x_hi, col)
    here_first = jnp.logical_and(first_to[0] == row, first_to[1] == col)
    here_second = mid_y == y
    y_up, y_down = same_col(at_row(y + 1, x_hi)), same_col(at_row(y + 3, x_hi))
    x_far = same_col(at_row(y, 1 - x_hi))
    z_up, z_down = same_row(at_k(x_lo, z + 1)), same_row(at_k(x_lo, z + 3))
    x_near = same_row(at_k(1 - x_lo, z))

    moves = [
        (lw_hbm, lw_ref),
        (rw_hbm, rw_ref),
        (align.at[:, pl.ds(0, 128)], x0),
        (align.at[:, pl.ds(128, 128)], x1),
        (gain_hbm, gain_ref),
        (offset_hbm, offset_ref),
        (pw_hbm, pw),
        (hw_hbm, hw_ref),
        (fw_hbm, fw_ref),
        (pair_hbm, pair),
        (pbias_hbm, pbias_ref),
        (pgain_hbm, pgain_ref),
        (poffset_hbm, poffset_ref),
        (hbias_hbm, hbias_ref),
        (fbias_hbm, fbias_ref),
    ]
    loads = [pltpu.make_async_copy(source, target, load_sem.at[at]) for at, (source, target) in enumerate(moves)]
    for load in loads:
        load.start()

    barrier = pltpu.get_barrier_semaphore()
    for device in (other_core, y_up, y_down, x_far, z_up, z_down, x_near):
        pl.semaphore_signal(barrier, inc=1, device_id=device, device_id_type=MESH)

    for device in (first_from, second_from):

        @pl.when(jnp.logical_or(device[0] != row, device[1] != col))
        def _(device=device):
            pl.semaphore_signal(barrier, inc=1, device_id=device, device_id_type=MESH)

    lane = lax.broadcasted_iota(jnp.int32, (256, 128), 1)
    loads[0].wait()
    loads[1].wait()
    for source, at in ((lw_ref, 0), (rw_ref, 128)):
        wide = jnp.concatenate([source[...]] * 4, axis=0).T
        for pos in range(4):
            placed = jnp.where(lane // 32 == pos, wide, 0.0)
            high, low = split(placed)
            wh[pl.ds(pos * 256, 256), pl.ds(at, 128)] = high
            wl[pl.ds(pos * 256, 256), pl.ds(at, 128)] = low

    for at in range(2, 6):
        loads[at].wait()

    gain = gain_ref[...]
    offset = offset_ref[...]

    def norm_body(g, carry):
        for pos in range(4):
            rows = pl.ds(g * 4 + pos, 64, stride=32)
            parts = center([x0[rows, :], x1[rows, :]], 256)
            for half in range(2):
                value = parts[half] * gain[:, half * 128 : half * 128 + 128] + offset[:, half * 128 : half * 128 + 128]
                high, low = split(value)
                at = pl.ds(pl.multiple_of(g * 64, 64), 64)
                xh[at, pl.ds(pos * 256 + half * 128, 128)] = high
                xl[at, pl.ds(pos * 256 + half * 128, 128)] = low
        return carry

    lax.fori_loop(0, 8, norm_body, 0)
    both = dot(xh[...], wh[...]) + dot(xl[...], wh[...]) + dot(xh[...], wl[...])
    for g in range(8):
        send_left[g // 2, :, pl.ds((g % 2) * 128, 128)] = both[g * 64 : g * 64 + 64, :128]
    for g in range(4):
        pair_rows = jnp.concatenate(
            [both[g * 64 : g * 64 + 64, 128:], both[g * 64 + 256 : g * 64 + 320, 128:]], axis=0
        )
        right[row, pl.ds(g * 128, 128), :] = pair_rows.T

    greeted = 7 + jnp.where(here_first, 0, 1) + jnp.where(here_second, 0, 1)
    pl.semaphore_wait(barrier, greeted)

    def r_copy(step, n, slot, device):
        block = right.at[slot, pl.ds(n * 128, 128), :]
        return pltpu.make_async_remote_copy(
            src_ref=block,
            dst_ref=block,
            send_sem=r_send.at[step, n],
            recv_sem=r_recv.at[step, n],
            device_id=device,
            device_id_type=MESH,
        )

    def l_copy(step, n, slot, device):
        block = left.at[n, core, slot]
        return pltpu.make_async_remote_copy(
            src_ref=block,
            dst_ref=block,
            send_sem=l_send.at[step, n],
            recv_sem=l_recv.at[step, n],
            device_id=device,
            device_id_type=MESH,
        )

    def c_copy(step, n, slot, half):
        block = left.at[n, half, slot]
        return pltpu.make_async_remote_copy(
            src_ref=block,
            dst_ref=block,
            send_sem=c_send.at[step, n],
            recv_sem=c_recv.at[step, n],
            device_id=other_core,
            device_id_type=MESH,
        )

    def first_copy(n):
        return pltpu.make_async_remote_copy(
            src_ref=send_left.at[n],
            dst_ref=passing.at[n],
            send_sem=t_send.at[0, n],
            recv_sem=t_recv.at[0, n],
            device_id=first_to,
            device_id_type=MESH,
        )

    def second_copy(n):
        return pltpu.make_async_remote_copy(
            src_ref=passing.at[n],
            dst_ref=left.at[n, core, mid_shard],
            send_sem=t_send.at[1, n],
            recv_sem=t_recv.at[1, n],
            device_id=second_to,
            device_id_type=MESH,
        )

    def first_arrival(n):
        return pltpu.make_async_copy(send_left.at[n], passing.at[n], t_recv.at[0, n])

    def second_arrival(n):
        return pltpu.make_async_copy(passing.at[n], left.at[n, core, shard], t_recv.at[1, n])

    def t_begin(n):
        @pl.when(jnp.logical_not(here_first))
        def _():
            first_copy(n).start()

        @pl.when(here_first)
        def _():
            first_arrival(n).start()

    def t_pass(n):
        first_arrival(n).wait()

        @pl.when(jnp.logical_not(here_second))
        def _():
            second_copy(n).start()

        @pl.when(here_second)
        def _():
            second_arrival(n).start()

    r_sent = [row, row, row, at_row(y, 1 - x_hi), at_row(y, 1 - x_hi), at_row(y + 3, x_hi), at_row(y + 1, 1 - x_hi)]
    r_to = [x_far, y_up, y_down, y_up, y_down, y_up, y_down]
    r_lands = [
        at_row(y, 1 - x_hi),
        at_row(y + 3, x_hi),
        at_row(y + 1, x_hi),
        at_row(y + 3, 1 - x_hi),
        at_row(y + 1, 1 - x_hi),
        at_row(y + 2, x_hi),
        at_row(y + 2, 1 - x_hi),
    ]
    x_other = 1 - x_lo
    l_sent = [
        shard,
        shard,
        shard,
        shard_at(x_other, z),
        shard_at(x_other, z),
        shard_at(x_lo, z + 3),
        shard_at(x_other, z + 1),
    ]
    l_to = [x_near, z_up, z_down, z_up, z_down, z_up, z_down]
    l_lands = [
        shard_at(x_other, z),
        shard_at(x_lo, z + 3),
        shard_at(x_lo, z + 1),
        shard_at(x_other, z + 3),
        shard_at(x_other, z + 1),
        shard_at(x_lo, z + 2),
        shard_at(x_other, z + 2),
    ]
    c_slots = [shard] + l_lands

    def r_start(step, n):
        r_copy(step, n, r_sent[step], r_to[step]).start()

    def r_wait(step, n):
        r_copy(step, n, r_lands[step], r_to[step]).wait_recv()

    def l_start(step, n):
        l_copy(step, n, l_sent[step], l_to[step]).start()

    def l_wait(step, n):
        l_copy(step, n, l_lands[step], l_to[step]).wait_recv()

    def c_start(step, n):
        c_copy(step, n, c_slots[step], core).start()

    def c_wait(step, n):
        c_copy(step, n, c_slots[step], 1 - core).wait_recv()

    def r_first(n):
        for step in (1, 2, 0):
            r_start(step, n)

    for n in range(CH):
        t_begin(n)
        r_first(n)

    for at in range(6, 9):
        loads[at].wait()

    def order_body(d, carry):
        high, low = split(pw[pl.ds(d, 32, stride=32), :])
        at = pl.ds(pl.multiple_of(d * 32, 32), 32)
        pwc[at, pl.ds(0, 128)] = high
        pwc[at, pl.ds(128, 128)] = low
        return carry

    lax.fori_loop(0, 32, order_body, 0)
    high, low = split(hw_ref[...])
    hwc[pl.ds(0, 128), :] = high
    hwc[pl.ds(128, 128), :] = high
    hwc[pl.ds(256, 128), :] = low
    high, low = split(fw_ref[...])
    fwc[:, pl.ds(0, 128)] = high
    fwc[:, pl.ds(128, 128)] = low

    def swap_first(n):
        t_pass(n)

    def swap_second(n):
        second_arrival(n).wait()
        for step in (1, 2, 0):
            l_start(step, n)
        c_start(0, n)

    def right_relay(step, further):
        def relay(n):
            r_wait(step, n)
            for later in further:
                r_start(later, n)

        return relay

    def left_relay(step, further):
        def relay(n):
            l_wait(step, n)
            for later in further:
                l_start(later, n)
            c_start(step + 1, n)

        return relay

    low_half = lax.broadcasted_iota(jnp.int32, (16, 128), 1) < 64

    def prepare(part):
        for n in range(CH):
            for step in ((), (3,), (2,), (5, 6))[part]:
                r_wait(step, n)
        p = (y + (0, 3, 1, 2)[part]) % 4

        def body(d, carry):
            a = right[2 * p, pl.ds(d, 16, stride=32), :]
            b = right[2 * p + 1, pl.ds(d, 16, stride=32), :]
            first = jnp.where(low_half, a, pltpu.roll(b, 64, 1))
            second = jnp.where(low_half, pltpu.roll(a, 64, 1), b)
            rows = pl.ds(pl.multiple_of(d * 32, 32), 32)
            high, low = split(jnp.concatenate([first, second], axis=0))
            lhs[rows, pl.ds(pl.multiple_of(p * 128, 128), 128)] = high
            lhs[rows, pl.ds(pl.multiple_of(512 + p * 128, 128), 128)] = low
            lhs[rows, pl.ds(pl.multiple_of(1024 + p * 128, 128), 128)] = high
            return carry

        lax.fori_loop(0, 32, body, 0, unroll=4)

    for at in range(9, 15):
        loads[at].wait()

    lane = lax.broadcasted_iota(jnp.int32, (32, 128), 1)
    below = lane < 64
    even = (lane // 32) % 2 == 0
    pbias, fbias, hbias = pbias_ref[...], fbias_ref[...], hbias_ref[...]
    pgain, poffset = pgain_ref[...], poffset_ref[...]

    def exchange_halves(a, b):
        moved = pltpu.roll(jnp.where(below, b, a), 64, 1)
        return jnp.where(below, a, moved), jnp.where(below, moved, b)

    def exchange_quarters(a, b):
        return jnp.where(even, a, pltpu.roll(b, 32, 1)), jnp.where(even, pltpu.roll(a, 96, 1), b)

    def outer(q):
        for h in range(2):
            high, low = split(left[q, h].reshape(512, 256))
            at = pl.ds(h * 256, 256)
            rhs[pl.ds(0, 512), at] = high
            rhs[pl.ds(512, 512), at] = high
            rhs[pl.ds(1024, 512), at] = low
        raw[q % 2] = dot(lhs[...], rhs[...])

    def finish(q):
        for t in range(8):
            for u in range(4):
                v = [raw[q % 2, pl.ds((4 * t + d) * 32, 32), pl.ds(u * 128, 128)] for d in range(4)]
                v[0], v[2] = exchange_halves(v[0], v[2])
                v[1], v[3] = exchange_halves(v[1], v[3])
                v[0], v[1] = exchange_quarters(v[0], v[1])
                v[2], v[3] = exchange_quarters(v[2], v[3])
                for i in range(4):
                    high, low = split(v[i])
                    oh[pl.ds((u * 4 + i) * 32, 32), pl.ds(t * 128, 128)] = high
                    ol[pl.ds((u * 4 + i) * 32, 32), pl.ds(t * 128, 128)] = low
        wide = dot(oh[...], pwc[...])
        update = wide[:, :128] + wide[:, 128:] + dot(ol[...], pwc[:, :128])
        tiles = [pl.ds((h * 32 + q * 8) * 32, 256) for h in range(2)]
        updated = jnp.concatenate([pair[rows, :] for rows in tiles], axis=0) + update * (1.0 / 512) + pbias
        (flat,) = center([updated], 128)
        high, low = split(flat * pgain + poffset)
        hidden = jnp.maximum(dot(jnp.concatenate([high, low, high], axis=1), hwc[...]) + hbias, 0.0)
        high, low = split(hidden)
        wide = dot(high, fwc[...])
        final = wide[:, :128] + wide[:, 128:] + dot(low, fwc[:, :128])
        result = updated + final + fbias
        for h in range(2):
            out[tiles[h], :] = result[h * 256 : h * 256 + 256]

    def store(q, h):
        rows = pl.ds(pl.multiple_of((h * 32 + q * 8) * 32, 256), 256)
        return pltpu.make_async_copy(out.at[rows, :], out_hbm.at[rows, :], out_sem.at[q * 2 + h])

    def arrive(q):
        for step in range(8):
            c_wait(step, q)

    def product(q):
        arrive(q)
        outer(q)

    def complete(q):
        finish(q)
        store(q, 0).start()
        store(q, 1).start()

    work = {
        "t1": swap_first,
        "t2": swap_second,
        "r0": right_relay(0, (3, 4)),
        "r1": right_relay(1, (5,)),
        "r4": right_relay(4, (6,)),
        "l0": left_relay(0, (3, 4)),
        "l1": left_relay(1, (5,)),
        "l2": left_relay(2, ()),
        "l3": left_relay(3, ()),
        "l4": left_relay(4, (6,)),
        "l5": left_relay(5, ()),
        "l6": left_relay(6, ()),
        "P": prepare,
        "O": product,
        "F": complete,
    }
    for name, n in ORDER:
        work[name](n)
    for n in range(CH):
        store(n, 0).wait()
        store(n, 1).wait()
    for n in range(CH):
        for step in range(7):
            r_copy(step, n, r_sent[step], r_to[step]).wait_send()
            l_copy(step, n, l_sent[step], l_to[step]).wait_send()
        for step in range(8):
            c_copy(step, n, c_slots[step], core).wait_send()

        @pl.when(jnp.logical_not(here_first))
        def _(n=n):
            first_copy(n).wait_send()

        @pl.when(jnp.logical_not(here_second))
        def _(n=n):
            second_copy(n).wait_send()


def on_device(
    alignment,
    align_gain,
    align_bias,
    left_weight,
    right_weight,
    project_weight,
    project_bias,
    pair_state,
    pair_gain,
    pair_bias,
    hidden_weight,
    hidden_bias,
    final_weight,
    final_bias,
):
    apart = pl.BlockSpec(memory_space=pl.ANY)
    dma = pltpu.SemaphoreType.DMA
    output = pl.pallas_call(
        kernel,
        out_shape=jax.ShapeDtypeStruct((2048, 128), F32),
        in_specs=[apart] * 14,
        out_specs=apart,
        scratch_shapes=[
            pltpu.VMEM((1, 256), F32),
            pltpu.VMEM((1, 256), F32),
            pltpu.VMEM((32, 256), F32),
            pltpu.VMEM((32, 256), F32),
            pltpu.VMEM((1, 128), F32),
            pltpu.VMEM((1, 128), F32),
            pltpu.VMEM((1, 128), F32),
            pltpu.VMEM((128, 512), F32),
            pltpu.VMEM((1, 512), F32),
            pltpu.VMEM((512, 128), F32),
            pltpu.VMEM((1, 128), F32),
            pltpu.VMEM((2048, 128), F32),
            pltpu.VMEM((2048, 128), F32),
            pltpu.VMEM((512, 1024), BF16),
            pltpu.VMEM((512, 1024), BF16),
            pltpu.VMEM((1024, 256), BF16),
            pltpu.VMEM((1024, 256), BF16),
            pltpu.VMEM((CH, 64, 256), F32),
            pltpu.VMEM((CH, 64, 256), F32),
            pltpu.VMEM((CH, 2, 8, 64, 256), F32),
            pltpu.VMEM((8, 512, 128), F32),
            pltpu.VMEM((1024, 1536), BF16),
            pltpu.VMEM((1536, 512), BF16),
            pltpu.VMEM((2, 1024, 512), F32),
            pltpu.VMEM((512, 1024), BF16),
            pltpu.VMEM((512, 1024), BF16),
            pltpu.VMEM((1024, 128), F32),
            pltpu.VMEM((1024, 256), BF16),
            pltpu.VMEM((384, 512), BF16),
            pltpu.VMEM((512, 256), BF16),
            pltpu.VMEM((2048, 128), F32),
            pltpu.VMEM((2048, 128), F32),
            dma((15,)),
            dma((7, CH)),
            dma((7, CH)),
            dma((7, CH)),
            dma((7, CH)),
            dma((8, CH)),
            dma((8, CH)),
            dma((2, CH)),
            dma((2, CH)),
            dma((8,)),
        ],
        compiler_params=pltpu.CompilerParams(
            collective_id=0, has_side_effects=True, vmem_limit_bytes=63 * 1024 * 1024
        ),
        cost_estimate=pl.CostEstimate(flops=10**10, bytes_accessed=6 * 10**6, transcendentals=0),
    )(
        alignment.reshape(2048, 256),
        align_gain.reshape(1, 256),
        align_bias.reshape(1, 256),
        left_weight.T,
        right_weight.T,
        project_weight,
        project_bias.reshape(1, 128),
        pair_state.reshape(2048, 128),
        pair_gain.reshape(1, 128),
        pair_bias.reshape(1, 128),
        hidden_weight,
        hidden_bias.reshape(1, 512),
        final_weight,
        final_bias.reshape(1, 128),
    )
    return output.reshape(64, 32, 128)


def solution(mesh):
    spread = P("row", "col", None)
    placed = (spread,) + (P(),) * 6 + (spread,) + (P(),) * 6
    return jax.shard_map(on_device, mesh=mesh, in_specs=placed, out_specs=spread, check_vma=False)
```

time: 95 us -> 67 us (0.71)
  the two profiles are of different devices: /device:TPU:10 before, /device:TPU:1 now
where the time goes in v1:
time: 67 us; the launch traced here: 66 us
  Pallas kernels  63.7 us (95%)
  local copies, waits for them, and re-layouts  2.26 us (3%)
    pallas_call x1, Pallas kernels, on_device(): pl.pallas_call(kernel, out_shape=jax.ShapeDtypeStruct((2048, 128), F32),...  63.7 us
    unnamed x1, local copies, waits for them, and re-layouts  2.26 us

profile of v1, /device:TPU:1, one launch (start us, length us, event | category | flops | bytes accessed | tf_op | source)
XLA Modules:
  0.0 66.0 jit_solution(517627576510011090)
XLA Ops:
  0.0 63.7 %shard_map.136 = f32[2048,128]{1,0:T(8,128)} custom-call(f32[2048,256]{1,0:T(8,128)} %bitcast.13, f32[1,256]{1,0:T(1,128)} %bitcast.18, f32[1,256]{1,0:T(1,128)} %bitcast.19, f32[32,256]{1,0:T(8,128)} %bitcast.15, f32[32,256]{1,0:T(8,128)} %bitcast.16, f32[1024,128]{1,0:T(8,128)} %pw_hbm.1, f32[1,128]{1,0:T(1,128)} %bitcast.20, f32[2048,128]{1,0:T(8,128)} %bitcast.14, ...), custom_call_target="tpu_custom_call" | custom-call | flops 10000000000 | bytes 6000000 | tf_op jit(solution)/shard_map/pallas_call | solution.py:552
  63.7 2.3 %copy.16 = f32[64,32,128]{2,1,0:T(8,128)} copy(f32[64,32,128]{2,1,0:T(8,128)} %bitcast.12) | data formatting | bytes 2097152

commit v2 on v1

--- a/solution.py
+++ b/solution.py
@@ -12,13 +12,13 @@
 MESH = pl.DeviceIdType.MESH
 CH = 4
 ORDER = (
-    ("r1", 0), ("t1", 0), ("r0", 0), ("r1", 1), ("t1", 1), ("r0", 1), ("r1", 2), ("t1", 2), ("r0", 2),
-    ("r1", 3), ("t2", 0), ("t1", 3), ("r0", 3), ("P", 0), ("t2", 1), ("r4", 0), ("t2", 2), ("r4", 1),
-    ("l1", 0), ("l2", 0), ("l0", 0), ("t2", 3), ("r4", 2), ("l1", 1), ("l2", 1), ("l0", 1), ("l1", 2),
-    ("l2", 2), ("l0", 2), ("r4", 3), ("P", 2), ("l5", 0), ("l4", 0), ("l0", 3), ("l3", 0), ("l2", 3),
-    ("l1", 3), ("l4", 1), ("l5", 1), ("l4", 2), ("P", 1), ("P", 3), ("l3", 1), ("l6", 0), ("l5", 2),
-    ("l4", 3), ("O", 0), ("l3", 2), ("l6", 1), ("F", 0), ("l3", 3), ("l6", 2), ("l5", 3), ("l6", 3), ("O", 1),
-    ("F", 1), ("O", 2), ("F", 2), ("O", 3), ("F", 3),
+    ("r0", 0), ("t1", 0), ("t1", 2), ("t1", 1), ("r0", 1), ("r0", 2), ("r0", 3), ("P", 0), ("t1", 3),
+    ("r1", 0), ("t2", 0), ("t2", 2), ("r1", 2), ("r4", 0), ("r1", 1), ("t2", 1), ("r4", 2), ("l0", 0),
+    ("l0", 2), ("r1", 3), ("r4", 3), ("r4", 1), ("l1", 0), ("l0", 1), ("l2", 2), ("l2", 0), ("l4", 0),
+    ("t2", 3), ("l3", 0), ("P", 2), ("P", 1), ("l1", 2), ("l1", 1), ("l5", 0), ("l4", 2), ("P", 3), ("l2", 1),
+    ("l3", 2), ("l6", 0), ("l4", 1), ("l3", 1), ("l0", 3), ("O", 0), ("F", 0), ("l5", 1), ("l6", 1),
+    ("l6", 2), ("l3", 3), ("l1", 3), ("l2", 3), ("l4", 3), ("l5", 2), ("O", 1), ("F", 1), ("l5", 3),
+    ("l6", 3), ("O", 2), ("F", 2), ("O", 3), ("F", 3),
 )
 
 
@@ -195,31 +195,6 @@
     gain = gain_ref[...]
     offset = offset_ref[...]
 
-    def norm_body(g, carry):
-        for pos in range(4):
-            rows = pl.ds(g * 4 + pos, 64, stride=32)
-            parts = center([x0[rows, :], x1[rows, :]], 256)
-            for half in range(2):
-                value = parts[half] * gain[:, half * 128 : half * 128 + 128] + offset[:, half * 128 : half * 128 + 128]
-                high, low = split(value)
-                at = pl.ds(pl.multiple_of(g * 64, 64), 64)
-                xh[at, pl.ds(pos * 256 + half * 128, 128)] = high
-                xl[at, pl.ds(pos * 256 + half * 128, 128)] = low
-        return carry
-
-    lax.fori_loop(0, 8, norm_body, 0)
-    both = dot(xh[...], wh[...]) + dot(xl[...], wh[...]) + dot(xh[...], wl[...])
-    for g in range(8):
-        send_left[g // 2, :, pl.ds((g % 2) * 128, 128)] = both[g * 64 : g * 64 + 64, :128]
-    for g in range(4):
-        pair_rows = jnp.concatenate(
-            [both[g * 64 : g * 64 + 64, 128:], both[g * 64 + 256 : g * 64 + 320, 128:]], axis=0
-        )
-        right[row, pl.ds(g * 128, 128), :] = pair_rows.T
-
-    greeted = 7 + jnp.where(here_first, 0, 1) + jnp.where(here_second, 0, 1)
-    pl.semaphore_wait(barrier, greeted)
-
     def r_copy(step, n, slot, device):
         block = right.at[slot, pl.ds(n * 128, 128), :]
         return pltpu.make_async_remote_copy(
@@ -354,9 +329,36 @@
         for step in (1, 2, 0):
             r_start(step, n)
 
-    for n in range(CH):
-        t_begin(n)
-        r_first(n)
+    for half in range(2):
+
+        def norm_body(g, carry, half=half):
+            group = half * 2 + (g // 2) * 4 + g % 2
+            for pos in range(4):
+                rows = pl.ds(group * 4 + pos, 64, stride=32)
+                parts = center([x0[rows, :], x1[rows, :]], 256)
+                for side in range(2):
+                    lanes = slice(side * 128, side * 128 + 128)
+                    high, low = split(parts[side] * gain[:, lanes] + offset[:, lanes])
+                    at = pl.ds(pl.multiple_of(g * 64, 64), 64)
+                    xh[half, at, pl.ds(pos * 256 + side * 128, 128)] = high
+                    xl[half, at, pl.ds(pos * 256 + side * 128, 128)] = low
+            return carry
+
+        lax.fori_loop(0, 4, norm_body, 0)
+        both = dot(xh[half], wh[...]) + dot(xl[half], wh[...]) + dot(xh[half], wl[...])
+        for g in range(4):
+            send_left[half + 2 * (g // 2), :, pl.ds((g % 2) * 128, 128)] = both[g * 64 : g * 64 + 64, :128]
+        if half == 0:
+            greeted = 7 + jnp.where(here_first, 0, 1) + jnp.where(here_second, 0, 1)
+            pl.semaphore_wait(barrier, greeted)
+        t_begin(half)
+        t_begin(half + 2)
+        for g in range(2):
+            pair_rows = jnp.concatenate(
+                [both[g * 64 : g * 64 + 64, 128:], both[g * 64 + 128 : g * 64 + 192, 128:]], axis=0
+            )
+            right[row, pl.ds((2 * half + g) * 128, 128), :] = pair_rows.T
+            r_first(2 * half + g)
 
     for at in range(6, 9):
         loads[at].wait()
@@ -568,8 +570,8 @@
             pltpu.VMEM((1, 128), F32),
             pltpu.VMEM((2048, 128), F32),
             pltpu.VMEM((2048, 128), F32),
-            pltpu.VMEM((512, 1024), BF16),
-            pltpu.VMEM((512, 1024), BF16),
+            pltpu.VMEM((2, 256, 1024), BF16),
+            pltpu.VMEM((2, 256, 1024), BF16),
             pltpu.VMEM((1024, 256), BF16),
             pltpu.VMEM((1024, 256), BF16),
             pltpu.VMEM((CH, 64, 256), F32),

time: 67 us -> 59.6 us (0.89); the launches traced: 66 us -> 59.5 us
  Pallas kernels: 63.7 us -> 57.2 us
    pallas_call x1, Pallas kernels: 63.7 us -> 57.2 us  [on_device(): pl.pallas_call(kernel, out_shape=jax.ShapeDtypeStruct((2048, 128), F32),...]
where the time goes in v2:
time: 59.6 us; the launch traced here: 59.5 us
  Pallas kernels  57.2 us (96%)
  local copies, waits for them, and re-layouts  2.26 us (4%)
    pallas_call x1, Pallas kernels, on_device(): pl.pallas_call(kernel, out_shape=jax.ShapeDtypeStruct((2048, 128), F32),...  57.2 us
    unnamed x1, local copies, waits for them, and re-layouts  2.26 us

profile of v2, /device:TPU:1, one launch (start us, length us, event | category | flops | bytes accessed | tf_op | source)
XLA Modules:
  0.0 59.5 jit_solution(16628429821614145758)
XLA Ops:
  0.0 57.2 %shard_map.136 = f32[2048,128]{1,0:T(8,128)} custom-call(f32[2048,256]{1,0:T(8,128)} %bitcast.13, f32[1,256]{1,0:T(1,128)} %bitcast.18, f32[1,256]{1,0:T(1,128)} %bitcast.19, f32[32,256]{1,0:T(8,128)} %bitcast.15, f32[32,256]{1,0:T(8,128)} %bitcast.16, f32[1024,128]{1,0:T(8,128)} %pw_hbm.1, f32[1,128]{1,0:T(1,128)} %bitcast.20, f32[2048,128]{1,0:T(8,128)} %bitcast.14, ...), custom_call_target="tpu_custom_call" | custom-call | flops 10000000000 | bytes 6000000 | tf_op jit(solution)/shard_map/pallas_call | solution.py:554
  57.2 2.3 %copy.16 = f32[64,32,128]{2,1,0:T(8,128)} copy(f32[64,32,128]{2,1,0:T(8,128)} %bitcast.12) | data formatting | bytes 2097152

commit v3 on v2

--- a/solution.py
+++ b/solution.py
@@ -12,13 +12,13 @@
 MESH = pl.DeviceIdType.MESH
 CH = 4
 ORDER = (
-    ("r0", 0), ("t1", 0), ("t1", 2), ("t1", 1), ("r0", 1), ("r0", 2), ("r0", 3), ("P", 0), ("t1", 3),
-    ("r1", 0), ("t2", 0), ("t2", 2), ("r1", 2), ("r4", 0), ("r1", 1), ("t2", 1), ("r4", 2), ("l0", 0),
-    ("l0", 2), ("r1", 3), ("r4", 3), ("r4", 1), ("l1", 0), ("l0", 1), ("l2", 2), ("l2", 0), ("l4", 0),
-    ("t2", 3), ("l3", 0), ("P", 2), ("P", 1), ("l1", 2), ("l1", 1), ("l5", 0), ("l4", 2), ("P", 3), ("l2", 1),
-    ("l3", 2), ("l6", 0), ("l4", 1), ("l3", 1), ("l0", 3), ("O", 0), ("F", 0), ("l5", 1), ("l6", 1),
-    ("l6", 2), ("l3", 3), ("l1", 3), ("l2", 3), ("l4", 3), ("l5", 2), ("O", 1), ("F", 1), ("l5", 3),
-    ("l6", 3), ("O", 2), ("F", 2), ("O", 3), ("F", 3),
+    ("r0", 0), ("t1", 0), ("t1", 2), ("t1", 1), ("t1", 3), ("r0", 2), ("r0", 3), ("r0", 1), ("r4", 0),
+    ("r1", 3), ("P", 0), ("t2", 0), ("r1", 0), ("t2", 2), ("t2", 1), ("l1", 0), ("r1", 1), ("r4", 2),
+    ("l2", 0), ("l0", 0), ("r4", 3), ("r1", 2), ("l1", 2), ("t2", 3), ("l2", 1), ("r4", 1), ("l1", 1),
+    ("l5", 0), ("l0", 2), ("P", 1), ("l0", 1), ("l2", 2), ("l3", 0), ("P", 2), ("l4", 0), ("l5", 2),
+    ("l0", 3), ("l5", 1), ("l2", 3), ("l6", 0), ("l1", 3), ("P", 3), ("l4", 2), ("O", 0), ("l6", 2),
+    ("l3", 2), ("l3", 1), ("l4", 1), ("l4", 3), ("F", 0), ("l5", 3), ("O", 2), ("l3", 3), ("l6", 1), ("F", 2),
+    ("l6", 3), ("O", 1), ("F", 1), ("O", 3), ("F", 3),
 )
 
 
@@ -292,10 +292,12 @@
         shard,
         shard_at(x_other, z),
         shard_at(x_other, z),
-        shard_at(x_lo, z + 3),
-        shard_at(x_other, z + 1),
+        None,
+        shard_at(x_lo, z + 2),
     ]
-    l_to = [x_near, z_up, z_down, z_up, z_down, z_up, z_down]
+    l_to = [x_near, z_up, z_down, z_up, z_down, None, x_near]
+    far_sent = (shard_at(x_lo, z + 3), shard_at(x_lo, z + 1))
+    far_to = (z_up, z_down)
     l_lands = [
         shard_at(x_other, z),
         shard_at(x_lo, z + 3),
@@ -313,11 +315,16 @@
     def r_wait(step, n):
         r_copy(step, n, r_lands[step], r_to[step]).wait_recv()
 
+    def l_sends(step, n):
+        if step == 5:
+            return l_copy(step, n, far_sent[n % 2], far_to[n % 2])
+        return l_copy(step, n, l_sent[step], l_to[step])
+
     def l_start(step, n):
-        l_copy(step, n, l_sent[step], l_to[step]).start()
+        l_sends(step, n).start()
 
     def l_wait(step, n):
-        l_copy(step, n, l_lands[step], l_to[step]).wait_recv()
+        l_copy(step, n, l_lands[step], x_near).wait_recv()
 
     def c_start(step, n):
         c_copy(step, n, c_slots[step], core).start()
@@ -401,6 +408,8 @@
             l_wait(step, n)
             for later in further:
                 l_start(later, n)
+            if step == 1 + n % 2:
+                l_start(5, n)
             c_start(step + 1, n)
 
         return relay
@@ -502,11 +511,11 @@
         "r1": right_relay(1, (5,)),
         "r4": right_relay(4, (6,)),
         "l0": left_relay(0, (3, 4)),
-        "l1": left_relay(1, (5,)),
+        "l1": left_relay(1, ()),
         "l2": left_relay(2, ()),
         "l3": left_relay(3, ()),
-        "l4": left_relay(4, (6,)),
-        "l5": left_relay(5, ()),
+        "l4": left_relay(4, ()),
+        "l5": left_relay(5, (6,)),
         "l6": left_relay(6, ()),
         "P": prepare,
         "O": product,
@@ -520,7 +529,7 @@
     for n in range(CH):
         for step in range(7):
             r_copy(step, n, r_sent[step], r_to[step]).wait_send()
-            l_copy(step, n, l_sent[step], l_to[step]).wait_send()
+            l_sends(step, n).wait_send()
         for step in range(8):
             c_copy(step, n, c_slots[step], core).wait_send()
 

time: 59.6 us -> 58.5 us (0.982)
  Pallas kernels: 57.2 us -> 56.1 us
    pallas_call x1, Pallas kernels: 57.2 us -> 56.1 us  [on_device(): pl.pallas_call(kernel, out_shape=jax.ShapeDtypeStruct((2048, 128), F32),...]
where the time goes in v3:
time: 58.5 us; the launch traced here: 58.4 us
  Pallas kernels  56.1 us (96%)
  local copies, waits for them, and re-layouts  2.26 us (4%)
    pallas_call x1, Pallas kernels, on_device(): pl.pallas_call(kernel, out_shape=jax.ShapeDtypeStruct((2048, 128), F32),...  56.1 us
    unnamed x1, local copies, waits for them, and re-layouts  2.26 us

profile of v3, /device:TPU:1, one launch (start us, length us, event | category | flops | bytes accessed | tf_op | source)
XLA Modules:
  0.0 58.4 jit_solution(671990753349409806)
XLA Ops:
  0.0 56.1 %shard_map.136 = f32[2048,128]{1,0:T(8,128)} custom-call(f32[2048,256]{1,0:T(8,128)} %bitcast.13, f32[1,256]{1,0:T(1,128)} %bitcast.18, f32[1,256]{1,0:T(1,128)} %bitcast.19, f32[32,256]{1,0:T(8,128)} %bitcast.15, f32[32,256]{1,0:T(8,128)} %bitcast.16, f32[1024,128]{1,0:T(8,128)} %pw_hbm.1, f32[1,128]{1,0:T(1,128)} %bitcast.20, f32[2048,128]{1,0:T(8,128)} %bitcast.14, ...), custom_call_target="tpu_custom_call" | custom-call | flops 10000000000 | bytes 6000000 | tf_op jit(solution)/shard_map/pallas_call | solution.py:563
  56.1 2.3 %copy.16 = f32[64,32,128]{2,1,0:T(8,128)} copy(f32[64,32,128]{2,1,0:T(8,128)} %bitcast.12) | data formatting | bytes 2097152

commit v4 on v3

--- a/solution.py
+++ b/solution.py
@@ -147,6 +147,16 @@
     z_up, z_down = same_row(at_k(x_lo, z + 1)), same_row(at_k(x_lo, z + 3))
     x_near = same_row(at_k(1 - x_lo, z))
 
+    barrier = pltpu.get_barrier_semaphore()
+    for device in (other_core, y_up, y_down, x_far, z_up, z_down, x_near):
+        pl.semaphore_signal(barrier, inc=1, device_id=device, device_id_type=MESH)
+
+    for device in (first_from, second_from):
+
+        @pl.when(jnp.logical_or(device[0] != row, device[1] != col))
+        def _(device=device):
+            pl.semaphore_signal(barrier, inc=1, device_id=device, device_id_type=MESH)
+
     moves = [
         (lw_hbm, lw_ref),
         (rw_hbm, rw_ref),
@@ -165,18 +175,8 @@
         (fbias_hbm, fbias_ref),
     ]
     loads = [pltpu.make_async_copy(source, target, load_sem.at[at]) for at, (source, target) in enumerate(moves)]
-    for load in loads:
-        load.start()
-
-    barrier = pltpu.get_barrier_semaphore()
-    for device in (other_core, y_up, y_down, x_far, z_up, z_down, x_near):
-        pl.semaphore_signal(barrier, inc=1, device_id=device, device_id_type=MESH)
-
-    for device in (first_from, second_from):
-
-        @pl.when(jnp.logical_or(device[0] != row, device[1] != col))
-        def _(device=device):
-            pl.semaphore_signal(barrier, inc=1, device_id=device, device_id_type=MESH)
+    for at in (2, 3, 0, 1, *range(4, 15)):
+        loads[at].start()
 
     lane = lax.broadcasted_iota(jnp.int32, (256, 128), 1)
     loads[0].wait()
@@ -351,7 +351,7 @@
                     xl[half, at, pl.ds(pos * 256 + side * 128, 128)] = low
             return carry
 
-        lax.fori_loop(0, 4, norm_body, 0)
+        lax.fori_loop(0, 4, norm_body, 0, unroll=2)
         both = dot(xh[half], wh[...]) + dot(xl[half], wh[...]) + dot(xh[half], wl[...])
         for g in range(4):
             send_left[half + 2 * (g // 2), :, pl.ds((g % 2) * 128, 128)] = both[g * 64 : g * 64 + 64, :128]

time: 58.5 us -> 58.4 us (level)
  no operation moved by 1% of the time
where the time goes in v4:
time: 58.4 us; the launch traced here: 58.3 us
  Pallas kernels  56 us (96%)
  local copies, waits for them, and re-layouts  2.26 us (4%)
    pallas_call x1, Pallas kernels, on_device(): pl.pallas_call(kernel, out_shape=jax.ShapeDtypeStruct((2048, 128), F32),...  56 us
    unnamed x1, local copies, waits for them, and re-layouts  2.26 us

profile of v4, /device:TPU:1, one launch (start us, length us, event | category | flops | bytes accessed | tf_op | source)
XLA Modules:
  0.0 58.3 jit_solution(14591110703254616314)
XLA Ops:
  0.0 56.0 %shard_map.136 = f32[2048,128]{1,0:T(8,128)} custom-call(f32[2048,256]{1,0:T(8,128)} %bitcast.13, f32[1,256]{1,0:T(1,128)} %bitcast.18, f32[1,256]{1,0:T(1,128)} %bitcast.19, f32[32,256]{1,0:T(8,128)} %bitcast.15, f32[32,256]{1,0:T(8,128)} %bitcast.16, f32[1024,128]{1,0:T(8,128)} %pw_hbm.1, f32[1,128]{1,0:T(1,128)} %bitcast.20, f32[2048,128]{1,0:T(8,128)} %bitcast.14, ...), custom_call_target="tpu_custom_call" | custom-call | flops 10000000000 | bytes 6000000 | tf_op jit(solution)/shard_map/pallas_call | solution.py:563
  56.0 2.3 %copy.16 = f32[64,32,128]{2,1,0:T(8,128)} copy(f32[64,32,128]{2,1,0:T(8,128)} %bitcast.12) | data formatting | bytes 2097152
